TPU v7x, 128 devices: a whole 4x4x4 slice. The times are simulated.
128 devices in a mesh: grid: 32 (over y, x, core), ao: 4 (over z).
Axes of the slice: x: 4, y: 4, z: 4, core: 2. Of those that a mesh axis runs over, the one named last changes fastest.
Arguments:
- colloc: bfloat16 [128, 128, 1024], P('grid', None, 'ao'), may hold values from -6 to 6
- potent: bfloat16 [128, 128, 1024], P('grid', None, 'ao'), may hold values from -6 to 6
- weights: float32 [128, 128], P('grid'), may hold values from 0.02 to 0.2
- density: bfloat16 [8192, 8192], P('grid'), may hold values from -0.1875 to 0.1875
- list_owner: int32 [128, 8], replicated, may hold values from 0 to 31, as said below
- list_local: int32 [128, 8], replicated, may hold values from 0 to 1
Outputs:
- exchange: float32 [8192, 8192], P('grid', 'ao')
Inputs may be any that keep to these rules, and one draw needn't show every extreme that they name: `list_owner`: each row names 8 different owners. Among the 4 rows of one index of grid (rows d * 4 to (d + 1) * 4 - 1), no owner is named by more than 2 rows.
All inputs are finite; a program needn't handle non-finite values.
Results may differ from a plain program's by a relative error of at most 0.0029.
Values may be sent and summed in bfloat16 or wider, within the bound.
A program may use at most 64 MiB of HBM per device.

v0:
```python
import jax
import jax.numpy as jnp
from jax import lax
from jax.sharding import PartitionSpec as P

RBS = 128
SIG = 8
RB_PER = 2


def owner_plan(owners, row_ids, local_rows, my_grid, my_part, capacity, per_part):
    n_grid = owners.shape[0]
    blocks = owners.shape[1]
    named_here = (owners == my_grid).astype(jnp.int32)
    counted = jnp.sum(named_here, axis=2)
    slot_of = jnp.sum(named_here * jnp.arange(SIG, dtype=jnp.int32), axis=2)
    before = jnp.cumsum(counted, axis=1) - counted
    places = jnp.arange(capacity, dtype=jnp.int32)
    chosen = ((counted[:, None, :] == 1) & (before[:, None, :] == places[None, :, None])).astype(
        jnp.int32
    )
    filled = jnp.sum(chosen, axis=2)
    which_block = jnp.sum(chosen * jnp.arange(blocks, dtype=jnp.int32), axis=2)
    which_slot = jnp.sum(chosen * slot_of[:, None, :], axis=2)
    readers = jnp.arange(n_grid, dtype=jnp.int32)[:, None]
    row_local = local_rows[readers, which_block, which_slot]
    wanted = my_part * per_part + jnp.arange(per_part, dtype=jnp.int32)
    col_blocks = row_ids[readers[:, :, None], which_block[:, :, None], wanted[None, None, :]]
    return (filled, row_local, col_blocks)


def reader_spots(mine, n_grid):
    onehot = (mine[:, :, None] == jnp.arange(n_grid, dtype=jnp.int32)).astype(jnp.int32)
    per_block = jnp.sum(onehot, axis=1)
    prior = jnp.cumsum(per_block, axis=0) - per_block
    return jnp.take_along_axis(prior, mine, axis=1)


def local(colloc, potent, weights, density, list_owner, list_local):
    n_grid = lax.axis_size("grid")
    n_ao = lax.axis_size("ao")
    my_grid = lax.axis_index("grid")
    my_part = lax.axis_index("ao")
    blocks = colloc.shape[0]
    per_part = SIG // n_ao
    width = per_part * RBS
    capacity = min(blocks, 2 * ((blocks * SIG + n_grid - 1) // n_grid))
    n_rows = density.shape[1] // RBS
    owners = list_owner.reshape(n_grid, blocks, SIG)
    local_rows = list_local.reshape(n_grid, blocks, SIG)
    row_ids = owners * RB_PER + local_rows
    filled, row_local, col_blocks = owner_plan(
        owners, row_ids, local_rows, my_grid, my_part, capacity, per_part
    )
    blocked = density.reshape(RB_PER, RBS, n_rows, RBS)
    tiles = blocked[row_local[:, :, None], :, col_blocks, :]
    tiles = jnp.where(filled[:, :, None, None, None] > 0, tiles, jnp.zeros_like(tiles))
    outgoing = jnp.transpose(tiles, (0, 1, 3, 2, 4)).reshape(n_grid, capacity, RBS, width)
    arrived = lax.all_to_all(outgoing, "grid", split_axis=0, concat_axis=0, tiled=True)
    whole_colloc = lax.all_gather(colloc, "ao", axis=2, tiled=True)
    mine = lax.dynamic_index_in_dim(owners, my_grid, 0, keepdims=False)
    spots = reader_spots(mine, n_grid)
    density_tiles = arrived[mine, spots].reshape(blocks, SIG * RBS, width)
    f_vals = jnp.einsum(
        "bpk,bkl->bpl", whole_colloc, density_tiles, preferred_element_type=jnp.float32
    )
    weighted = (weights[:, :, None] * potent * f_vals).astype(jnp.bfloat16)
    partial_tiles = jnp.einsum(
        "bpk,bpl->bkl", whole_colloc, weighted, preferred_element_type=jnp.float32
    )
    partial_tiles = partial_tiles.reshape(blocks, SIG, RBS, width)
    sending = (
        jnp.zeros((n_grid, capacity, RBS, width), jnp.float32).at[mine, spots].set(partial_tiles)
    )
    incoming = lax.all_to_all(sending, "grid", split_axis=0, concat_axis=0, tiled=True)
    pieces = jnp.transpose(incoming.reshape(n_grid, capacity, RBS, per_part, RBS), (0, 1, 3, 2, 4))
    totals = jnp.zeros((RB_PER, RBS, n_rows, RBS), jnp.float32)
    totals = totals.at[row_local[:, :, None], :, col_blocks, :].add(pieces)
    flat = totals.reshape(RB_PER * RBS, n_rows * RBS)
    return lax.psum_scatter(flat, "ao", scatter_dimension=1, tiled=True)


def solution(mesh):
    placed = (
        P("grid", None, "ao"),
        P("grid", None, "ao"),
        P("grid", None),
        P("grid", None),
        P(),
        P(),
    )
    return jax.shard_map(
        local, mesh=mesh, in_specs=placed, out_specs=P("grid", "ao"), check_vma=False
    )
```

profile of v0, /device:TPU:1, one launch (start us, length us, event | category | flops | bytes accessed | tf_op | source)
XLA Modules:
  0.0 384.8 jit_solution(3332487736202820021)
XLA Ops:
  6.5 0.7 select_reduce_fusion.1
  7.6 0.2 reduce_window_sum.22
  8.2 0.8 copy.84
  9.0 1.0 gather_fusion
  10.6 0.1 reshape.210
  11.1 1.2 gather_fusion.1
  12.3 0.2 gather.22
  12.6 0.1 reshape.216
  12.8 3.4 copy.109
  16.2 4.6 %copy.100 = bf16[2,128,64,128]{3,1,2,0:T(8,128)(2,1)} copy(bf16[2,128,64,128]{3,2,1,0:T(8,128)(2,1)S(1)} %bitcast.74) | data formatting | bytes 8388608 | tf_op jit(solution)/shard_map/reshape | solution.py:55
  20.8 5.3 %gather_fusion.2 = bf16[128,128,128]{2,1,0:T(8,128)(2,1)} fusion(bf16[2,128,64,128]{3,1,2,0:T(8,128)(2,1)} %copy.100, s32[128]{0:T(128)S(1)} %reshape.216), kind=kCustom, calls=%fused_computation.2 | custom fusion | bytes 8389632 | tf_op jit(solution)/shard_map/gather | solution.py:56
  26.1 5.7 %copy_bitcast_fusion.1 = bf16[32,2,128,256]{3,2,1,0:T(8,128)(2,1)} fusion(bf16[32,2,2,128,128]{4,3,2,1,0:T(8,128)(2,1)} %bitcast.75, pred[32,2]{1,0:T(8,128)(4,1)S(1)} %copy.99), kind=kLoop, calls=%fused_computation.8 | loop fusion | flops 2097152 | bytes 8388672 | tf_op jit(solution)/shard_map/reshape | solution.py:58
  31.8 8.8 %all-to-all-start = ((bf16[32,2,128,256]{3,2,1,0:T(8,128)(2,1)}), bf16[32,2,128,256]{3,2,1,0:T(8,128)(2,1)}, u32[]{:S(2)}, u32[]{:S(2)}) async-start(bf16[32,2,128,256]{3,2,1,0:T(8,128)(2,1)} %copy_bitcast_fusion.1), calls=%async_computation | async-start | bytes 8388608 | tf_op jit(solution)/shard_map/all_to_all | solution.py:59
  40.6 0.7 all-gather.2.cloned.1.call-update
  41.6 0.8 gather_fusion.4
  42.6 0.2 copy.98
  42.8 48.1 %all-to-all-done = bf16[32,2,128,256]{3,2,1,0:T(8,128)(2,1)} async-done(((bf16[32,2,128,256]{3,2,1,0:T(8,128)(2,1)}), bf16[32,2,128,256]{3,2,1,0:T(8,128)(2,1)}, u32[]{:S(2)}, u32[]{:S(2)}) %all-to-all-start) | async-done | bytes 4194336 | tf_op jit(solution)/shard_map/all_to_all | solution.py:59
  90.8 2.9 gather_fusion.3
  93.8 5.0 %convolution_bitcast_fusion = f32[4,1024,256]{1,2,0:T(8,128)} fusion(bf16[4,128,1024]{2,1,0:T(8,128)(2,1)} %all-gather.2.cloned.1.call-done, bf16[4,1024,256]{2,1,0:T(8,128)(2,1)S(1)} %bitcast.76, bf16[4,128,256]{1,2,0:T(8,128)(2,1)S(1)} %copy.98, f32[4,128]{1,0:T(4,128)S(1)} %copy-done.2), kind=kOutput, calls=%fused_computation.10 | convolution fusion | flops 537395200 | bytes 7604224 | tf_op jit(solution)/shard_map/bpk,bpl->bkl/dot_general | solution.py:68
  98.8 5.4 %copy.103 = f32[4,1024,256]{2,1,0:T(8,128)} copy(f32[4,1024,256]{1,2,0:T(8,128)} %convolution_bitcast_fusion) | data formatting | bytes 8388608 | tf_op jit(solution)/shard_map/bpk,bpl->bkl/dot_general | solution.py:68
  104.2 4.2 %broadcast_in_dim.30 = f32[32,2,128,256]{3,2,1,0:T(8,128)} broadcast(f32[]{:T(128)} %constant.20.clone.1), dimensions={} | broadcast | bytes 8388612 | tf_op jit(solution)/shard_map/broadcast_in_dim | solution.py:73
  108.4 8.6 %scatter_fusion = f32[32,2,128,256]{3,2,1,0:T(8,128)} fusion(f32[32,2,128,256]{3,2,1,0:T(8,128)} %broadcast_in_dim.30, s32[32]{0:T(128)S(1)} %reshape.234, f32[32,128,256]{2,1,0:T(8,128)} %bitcast.73), kind=kCustom, calls=%fused_computation.5 | custom fusion | bytes 12583168 | tf_op jit(solution)/shard_map/scatter | solution.py:73
  117.0 8.1 %all-to-all-start.1 = ((f32[32,2,128,256]{3,2,1,0:T(8,128)}), f32[32,2,128,256]{3,2,1,0:T(8,128)}, u32[]{:S(2)}, u32[]{:S(2)}) async-start(f32[32,2,128,256]{3,2,1,0:T(8,128)} %scatter_fusion), calls=%async_computation.1 | async-start | bytes 16777216 | tf_op jit(solution)/shard_map/all_to_all | solution.py:75
  125.2 0.1 reshape.240
  125.3 99.6 %all-to-all-done.1 = f32[32,2,128,256]{3,2,1,0:T(8,128)} async-done(((f32[32,2,128,256]{3,2,1,0:T(8,128)}), f32[32,2,128,256]{3,2,1,0:T(8,128)}, u32[]{:S(2)}, u32[]{:S(2)}) %all-to-all-start.1) | async-done | bytes 8388640 | tf_op jit(solution)/shard_map/all_to_all | solution.py:75
  224.9 8.9 %copy.104 = f32[32,2,128,256]{2,3,1,0:T(8,128)} copy(f32[32,2,128,256]{3,2,1,0:T(8,128)} %all-to-all-done.1) | data formatting | bytes 16777216 | tf_op jit(solution)/shard_map/all_to_all | solution.py:75
  233.8 9.0 %copy.105 = f32[128,128,128]{2,1,0:T(8,128)} copy(f32[128,128,128]{1,2,0:T(8,128)} %bitcast.71) | data formatting | bytes 16777216 | tf_op jit(solution)/shard_map/transpose | solution.py:76
  242.8 4.3 %broadcast_in_dim.24 = f32[2,128,64,128]{3,1,2,0:T(8,128)} broadcast(f32[]{:T(128)} %constant.20.clone.1), dimensions={} | broadcast | bytes 8388612 | tf_op jit(solution)/shard_map/broadcast_in_dim | solution.py:77
  247.1 27.0 %scatter_fusion.1 = f32[2,128,64,128]{3,1,2,0:T(8,128)} fusion(f32[2,128,64,128]{3,1,2,0:T(8,128)} %broadcast_in_dim.24, s32[128]{0:T(128)S(1)} %reshape.240, f32[128,128,128]{2,1,0:T(8,128)} %copy.105), kind=kCustom, calls=%fused_computation.6 | custom fusion | flops 2097152 | bytes 25166848 | tf_op jit(solution)/shard_map/scatter-add | solution.py:78
  274.1 8.2 %copy.106 = f32[2,128,64,128]{3,2,1,0:T(8,128)S(1)} copy(f32[2,128,64,128]{3,1,2,0:T(8,128)} %scatter_fusion.1) | data formatting | bytes 16777216 | tf_op jit(solution)/shard_map/scatter-add | solution.py:78
  282.3 10.9 %copy.113 = f32[32,8,64,128]{3,1,2,0:T(8,128)} copy(f32[32,8,64,128]{3,2,1,0:T(8,128)S(1)} %bitcast.72) | data formatting | bytes 16777216
  293.2 84.7 %reduce-scatter.2.cloned.1.call-done = f32[256,2048]{1,0:T(8,128)} async-done(((f32[256,8192]{1,0:T(8,128)}), f32[256,2048]{1,0:T(8,128)}) %reduce-scatter.2.cloned.1.call-update) | async-done | bytes 2097168 | tf_op jit(solution)/shard_map/reduce_scatter | solution.py:80
  (48 shorter events, 2.4 us)
Async XLA Ops:
  9.0 1.2 copy-start.1
  31.8 10.8 %copy-start = (bf16[4,128,256]{2,1,0:T(8,128)(2,1)S(1)}, bf16[4,128,256]{2,1,0:T(8,128)(2,1)}, u32[]{:S(2)}) copy-start(bf16[4,128,256]{2,1,0:T(8,128)(2,1)} %param.7) | copy-start | bytes 786436
  31.8 59.0 %all-to-all-start = ((bf16[32,2,128,256]{3,2,1,0:T(8,128)(2,1)}), bf16[32,2,128,256]{3,2,1,0:T(8,128)(2,1)}, u32[]{:S(2)}, u32[]{:S(2)}) async-start(bf16[32,2,128,256]{3,2,1,0:T(8,128)(2,1)} %copy_bitcast_fusion.1), calls=%async_computation | async-start | bytes 8388608 | tf_op jit(solution)/shard_map/all_to_all | solution.py:59
  40.6 53.2 %copy-start.2 = (f32[4,128]{1,0:T(4,128)S(1)}, f32[4,128]{1,0:T(4,128)}, u32[]{:S(2)}) copy-start(f32[4,128]{1,0:T(4,128)} %param.8) | copy-start | bytes 6148
  40.6 53.2 %all-gather.2.cloned.1.call-start = ((), (), s32[]{:S(2)}) async-start(), calls=%async_computation.3 | async-start | bytes 1310720 | tf_op jit(solution)/shard_map/all_gather | solution.py:60
  117.0 107.9 %all-to-all-start.1 = ((f32[32,2,128,256]{3,2,1,0:T(8,128)}), f32[32,2,128,256]{3,2,1,0:T(8,128)}, u32[]{:S(2)}, u32[]{:S(2)}) async-start(f32[32,2,128,256]{3,2,1,0:T(8,128)} %scatter_fusion), calls=%async_computation.1 | async-start | bytes 16777216 | tf_op jit(solution)/shard_map/all_to_all | solution.py:75
  125.1 252.9 %reduce-scatter.2.cloned.1.call-start = ((), (), s32[]{:S(2)}) async-start(), calls=%async_computation.4 | async-start | bytes 10485760 | tf_op jit(solution)/shard_map/reduce_scatter | solution.py:80
Sparse Core Ops, SparseCore 0:
  43.1 27.2 all-gather.1
  293.4 84.5 reduce-scatter.1
where the time goes:
time: 386 us; the launch traced here: 385 us
  waiting for transfers between devices  233 us (60%)
  local copies, waits for them, and re-layouts  82 us (21%)
  other arithmetic  34.1 us (9%)
  starting transfers between devices  17 us (4%)
  between operations  13.6 us (4%)
  matrix products  5.01 us (1%)
    all_to_all x1, waiting for transfers between devices, local(): lax.all_to_all(sending, 'grid', split_axis=0, concat_axis=0, tiled=True)  99.6 us
    reduce_scatter x1, waiting for transfers between devices, local(): return lax.psum_scatter(flat, 'ao', scatter_dimension=1, tiled=True)  84.7 us
    all_to_all x1, waiting for transfers between devices, local(): lax.all_to_all(outgoing, 'grid', split_axis=0, concat_axis=0, tiled=True)  48.1 us
    scatter-add x1, other arithmetic, local(): totals = totals.at[row_local[:, :, None], :, col_blocks, :].add(pieces)  27 us
    unnamed x11, local copies, waits for them, and re-layouts  15.3 us
    transpose x1, local copies, waits for them, and re-layouts, local(): jnp.transpose(incoming.reshape(n_grid, capacity, RBS, per_part, RBS), (0,...  9 us
    all_to_all x1, local copies, waits for them, and re-layouts, local(): lax.all_to_all(sending, 'grid', split_axis=0, concat_axis=0, tiled=True)  8.95 us
    all_to_all x1, starting transfers between devices, local(): lax.all_to_all(outgoing, 'grid', split_axis=0, concat_axis=0, tiled=True)  8.78 us
  transfers between devices with their start and end apart: 4, of which 3 were waited for; matrix products, arithmetic and copies ran while one was open for 1% of the time, Pallas kernels for 0%

commit v1 on v0

v1 whole, which is shorter than its diff:
```python
import functools

import jax
import jax.numpy as jnp
from jax import lax
from jax.experimental import pallas as pl
from jax.experimental.pallas import tpu as pltpu
from jax.sharding import PartitionSpec as P

RBS = 128
SIG = 8
BLK = 4
NG = 32
NA = 4
NY = 4
NX = 4
CAP = 2
TILES = 16
N_COL = 64
MESH = pl.DeviceIdType.MESH
F32 = jnp.float32
BF16 = jnp.bfloat16

T_K0 = 0
T_K1 = T_K0 + NG * CAP
T_ARR = T_K1 + NG * CAP
T_CB = T_ARR + BLK * SIG
T_SEL = T_CB + NG * CAP
T_IDX = T_SEL + TILES
T_END = T_IDX + NG * CAP * TILES

OFFSETS = sorted(
    [(oy, ox, oc) for oy in range(NY) for ox in range(NX) for oc in range(2) if (oy, ox, oc) != (0, 0, 0)],
    key=lambda o: -(min(o[0], NY - o[0]) + min(o[1], NX - o[1])),
)


def plan(list_owner, list_local, me, part):
    owners = list_owner.reshape(NG, BLK, SIG)
    local_rows = list_local.reshape(NG, BLK, SIG)
    row_ids = owners * 2 + local_rows
    i32 = jnp.int32
    places = jnp.arange(CAP, dtype=i32)
    lower = (jnp.arange(BLK)[:, None] > jnp.arange(BLK)[None, :]).astype(i32)

    hit = (owners == me).astype(i32)
    named = jnp.sum(hit, axis=2)
    before = jnp.sum(named[:, None, :] * lower[None], axis=2)
    chosen = named[:, None, :] * (before[:, None, :] == places[None, :, None]).astype(i32)
    valid = jnp.sum(chosen, axis=2)
    row = jnp.sum(chosen * jnp.sum(hit * local_rows, axis=2)[:, None, :], axis=2)
    my_cols = lax.dynamic_slice_in_dim(row_ids, part * 2, 2, axis=2)
    cols = jnp.sum(chosen[:, :, :, None] * my_cols[:, None], axis=2)
    keep = (valid[:, :, None] * (row[:, :, None] == jnp.arange(2, dtype=i32))).astype(F32)

    mine = lax.dynamic_index_in_dim(owners, me, 0, keepdims=False)
    mine_named = jnp.sum((mine[:, :, None] == jnp.arange(NG, dtype=i32)).astype(i32), axis=1)
    mine_before = jnp.sum(mine_named[None] * lower[:, :, None], axis=1)
    same = (mine[:, :, None] == jnp.arange(NG, dtype=i32)).astype(i32)
    spot = jnp.sum(same * mine_before[:, None, :], axis=2)
    arr = mine * CAP + spot

    pick = mine_named[None] * (mine_before[None] == places[:, None, None]).astype(i32)
    cb = jnp.sum(pick * jnp.arange(BLK, dtype=i32)[None, :, None], axis=1)
    slot = jnp.sum(same * jnp.arange(SIG, dtype=i32)[None, :, None], axis=1)
    cj = jnp.sum(pick * slot[None], axis=1)
    cb = (cj // 2) * (2 * BLK) + cb * 2 + cj % 2

    group = (owners // (NG // NA) == part).astype(i32).reshape(NG, BLK * SIG)
    n = BLK * SIG
    below = (jnp.arange(n)[:, None] > jnp.arange(n)[None, :]).astype(i32)
    rank = jnp.sum(group[:, None, :] * below[None], axis=2)
    my_group = lax.dynamic_index_in_dim(group, me, 0, keepdims=False)
    my_rank = lax.dynamic_index_in_dim(rank, me, 0, keepdims=False)
    flat = jnp.arange(n, dtype=i32)
    b_of, k_of = flat // SIG, flat % SIG
    stored = (k_of // 2) * (2 * BLK) + b_of * 2 + k_of % 2
    tiles = jnp.arange(TILES, dtype=i32)
    sel = jnp.sum(my_group[None] * (my_rank[None] == tiles[:, None]).astype(i32) * stored[None], axis=1)

    here = (row_ids[:, :, :, None] == part * TILES + tiles).astype(i32)
    at = jnp.sum(here * (rank.reshape(NG, BLK, SIG)[..., None] - TILES), axis=2)
    idx = TILES + jnp.sum(chosen[..., None] * at[:, None], axis=2)

    tab = jnp.concatenate(
        [
            (row * N_COL + cols[:, :, 0]).reshape(-1),
            (row * N_COL + cols[:, :, 1]).reshape(-1),
            arr.reshape(-1),
            cb.T.reshape(-1),
            sel,
            idx.reshape(-1),
        ]
    )
    return tab, keep.reshape(-1)


def kernel(tab, keep, colloc, potent, weights, dens, out, dtiles, send, arrived, cfull, cqs, cown, wz, lhs_t, picked, *rest):
    held = rest[: NG]
    dsend, drecv, csend, crecv, zsend, zrecv, gsend, grecv = rest[NG:]
    me = lax.axis_index("grid")
    part = lax.axis_index("ao")
    y = me // (2 * NX)
    x = (me // 2) % NX
    core = me % 2

    def at_offset(oy, ox, oc):
        return ((y + oy + NY) % NY) * (2 * NX) + ((x + ox + NX) % NX) * 2 + (core + oc) % 2

    barrier = pltpu.get_barrier_semaphore()
    for o in OFFSETS:
        pl.semaphore_signal(barrier, inc=1, device_id=(at_offset(*o), part), device_id_type=MESH)
    for o in range(1, NA):
        pl.semaphore_signal(barrier, inc=1, device_id=(me, (part + o) % NA), device_id_type=MESH)

    def pack(d, carry):
        for c in range(CAP):
            i = d * CAP + c
            for h, base in enumerate((T_K0, T_K1)):
                send[i, :, h * RBS : (h + 1) * RBS] = dtiles[tab[base + i]]
        return carry

    for r in range(2):
        for k in range(N_COL):
            dtiles[r * N_COL + k] = dens[r * RBS : (r + 1) * RBS, k * RBS : (k + 1) * RBS]
    lax.fori_loop(0, NG, pack, 0)
    for b in range(BLK):
        for h in range(2):
            cfull[part * 2 * BLK + 2 * b + h] = colloc[b, :, h * RBS : (h + 1) * RBS]
    pl.semaphore_wait(barrier, len(OFFSETS) + NA - 1)

    def z_copy(buf, base, o, there):
        count = buf.shape[0] // NA
        return pltpu.make_async_remote_copy(
            src_ref=buf.at[pl.ds(part * count, count)],
            dst_ref=buf.at[pl.ds(there * count, count)],
            send_sem=zsend.at[base + o - 1],
            recv_sem=zrecv.at[base + o - 1],
            device_id=(me, (part + o) % NA),
            device_id_type=MESH,
        )

    def z_start(buf, base):
        for o in (2, 1, 3):
            z_copy(buf, base, o, part).start()

    def z_wait_recv(buf, base):
        for o in (1, 3, 2):
            z_copy(buf, base, o, (part + NA - o) % NA).wait_recv()

    def z_wait_send(buf, base):
        for o in (1, 2, 3):
            z_copy(buf, base, o, part).wait_send()

    def d_copy(n, c, recv):
        oy, ox, oc = OFFSETS[n]
        to = at_offset(oy, ox, oc)
        frm = at_offset(-oy, -ox, oc) if recv else me
        return pltpu.make_async_remote_copy(
            src_ref=send.at[to * CAP + c],
            dst_ref=arrived.at[frm * CAP + c],
            send_sem=dsend.at[n * CAP + c],
            recv_sem=drecv.at[n * CAP + c],
            device_id=(to, part),
            device_id_type=MESH,
        )

    def c_copy(n, recv):
        oy, ox, oc = OFFSETS[n]
        to = at_offset(oy, ox, oc)
        frm = at_offset(-oy, -ox, oc) if recv else me
        return pltpu.make_async_remote_copy(
            src_ref=cqs.at[to],
            dst_ref=cown.at[part * NG + frm],
            send_sem=csend.at[n],
            recv_sem=crecv.at[n],
            device_id=(to, part),
            device_id_type=MESH,
        )

    z_start(cfull, 0)
    for n in range(NG - 1):
        d_copy(n, 0, False).start()
    for c in range(CAP):
        arrived[me * CAP + c] = send[me * CAP + c]

    z_wait_recv(cfull, 0)
    quarter = RBS // NA

    def pack_c(o, carry):
        for c in range(CAP):
            picked[...] = cfull[tab[T_CB + o * CAP + c]]
            rows = pl.multiple_of(part * quarter, quarter)
            cqs[o, c] = picked[pl.ds(rows, quarter), :]
        return carry

    lax.fori_loop(0, NG, pack_c, 0)
    for n in range(NG - 1):
        c_copy(n, False).start()
    for n in range(NG - 1):
        d_copy(n, 1, False).start()
    cown[part * NG + me] = cqs[me]
    for s in range(NG):
        held[s][TILES] = jnp.zeros((RBS, RBS), BF16)
    for n in range(NG - 1):
        c_copy(n, True).wait_recv()
    z_start(cown, 3)
    for c in range(CAP):
        for n in range(NG - 1):
            d_copy(n, c, True).wait_recv()

    for b in range(BLK):
        left = jnp.concatenate([cfull[q * 2 * BLK + 2 * b + h] for q in range(NA) for h in range(2)], axis=1)
        right = jnp.concatenate([arrived[tab[T_ARR + b * SIG + j]] for j in range(SIG)], axis=0)
        f_vals = jnp.dot(left, right, preferred_element_type=F32)
        w = jnp.transpose(jnp.broadcast_to(weights[b : b + 1, :], (RBS, RBS)))
        for h in range(2):
            cut = slice(h * RBS, (h + 1) * RBS)
            wz[part * 2 * BLK + 2 * b + h] = (w * potent[b, :, cut].astype(F32) * f_vals[:, cut]).astype(BF16)
    z_start(wz, 6)

    z_wait_recv(cown, 3)

    def build(d, carry):
        for c in range(CAP):
            tile = jnp.concatenate([cown[q * NG + d, c].astype(F32) for q in range(NA)], axis=0)
            tile = jnp.transpose(tile)
            for r in range(2):
                lhs_t[d, r * RBS : (r + 1) * RBS, c * RBS : (c + 1) * RBS] = (
                    tile * keep[(d * CAP + c) * 2 + r]
                ).astype(BF16)
        return carry

    lax.fori_loop(0, NG, build, 0)
    out[...] = jnp.zeros_like(out)
    z_wait_recv(wz, 6)

    def piece(oy, ox, oc=0):
        return held[((oy % NY) * NX + ox % NX) * 2 + oc]

    own = piece(0, 0)
    for t in range(TILES):
        own[t] = wz[tab[T_SEL + t]]

    moves = {}

    def move(key, oy, ox, low, count, dy, dx, dc=0):
        n = len(moves)
        rows = pl.ds(low, count)
        copy = pltpu.make_async_remote_copy(
            src_ref=piece(oy, ox).at[rows],
            dst_ref=piece(oy + dy, ox + dx, dc).at[rows],
            send_sem=gsend.at[n],
            recv_sem=grecv.at[n],
            device_id=(at_offset(dy, dx, dc), part),
            device_id_type=MESH,
        )
        moves[key] = copy
        copy.start()

    first = ((0, 1), (1, 0))
    second = ((1, 0), (0, 1))
    half = TILES // 2

    def along(h, i, s=0):
        (py, px), (qy, qx) = first[h], second[h]
        return (i * py + s * qy, i * px + s * qx)

    def send_first(h):
        for s in (1, -1):
            move(("p", h, s), 0, 0, h * half, half, *along(h, s))

    def send_second(h, i):
        for s in (1, -1):
            move(("q", h, i, s), *along(h, i), h * half, half, *along(h, 0, s))

    def split(h, s):
        return h * half + (0 if s > 0 else half // 2), half // 2

    def forward_first(h, s):
        moves["p", h, s].wait_recv()
        move(("pf", h, s), *along(h, s), *split(h, s), *along(h, s))

    def forward_second(h, i, s):
        moves["q", h, i, s].wait_recv()
        move(("qf", h, i, s), *along(h, i, s), *split(h, s), *along(h, 0, s))

    def to_sibling(oy, ox):
        move(("s", oy % NY, ox % NX), oy, ox, 0, TILES, 0, 0, 1)

    def add_piece(oy, ox, oc):
        src = at_offset(-oy, -ox, oc)
        buf = piece(oy, ox, oc)
        width = 4

        def step(m, carry):
            tiles = []
            for c in range(CAP):
                base = T_IDX + (src * CAP + c) * TILES + m * width
                tiles.append(jnp.concatenate([buf[tab[base + w]] for w in range(width)], axis=1))
            right = jnp.concatenate(tiles, axis=0)
            cols = pl.ds(pl.multiple_of(m * width * RBS, width * RBS), width * RBS)
            out[:, cols] += jnp.dot(lhs_t[src], right, preferred_element_type=F32)
            return carry

        lax.fori_loop(0, TILES // width, step, 0)

    def finish(pieces):
        for oy, ox in pieces:
            to_sibling(oy, ox)

    def add(pieces, oc):
        for oy, ox in pieces:
            if oc:
                moves["s", oy % NY, ox % NX].wait_recv()
            add_piece(oy, ox, oc)

    for h in range(2):
        send_first(h)
    for h in range(2):
        send_second(h, 0)
    to_sibling(0, 0)
    add([(0, 0)], 0)
    for s in (1, -1):
        for h in range(2):
            forward_first(h, s)
            send_second(h, s)
    for s in (1, -1):
        for h in range(2):
            forward_second(h, 0, s)
    near = [(0, 1), (0, -1), (1, 0), (-1, 0)]
    finish(near)
    for h in range(2):
        for s in (1, -1):
            moves["pf", h, s].wait_recv()
        send_second(h, 2)
    add([(0, 0)], 1)
    add(near, 0)
    diagonal = [(1, 1), (1, -1), (-1, 1), (-1, -1)]
    for i in (1, -1):
        for s in (1, -1):
            for h in range(2):
                forward_second(h, i, s)
    finish(diagonal)
    for h in range(2):
        for s in (1, -1):
            moves["qf", h, 0, s].wait_recv()
    straight = [(0, 2), (2, 0)]
    finish(straight)
    add(near, 1)
    add(diagonal, 0)
    for s in (1, -1):
        for h in range(2):
            forward_second(h, 2, s)
    add(straight, 0)
    add(diagonal, 1)
    for i in (1, -1):
        for h in range(2):
            for s in (1, -1):
                moves["qf", h, i, s].wait_recv()
    knight = [(1, 2), (-1, 2), (2, 1), (2, -1)]
    finish(knight)
    add(straight, 1)
    add(knight, 0)
    for h in range(2):
        for s in (1, -1):
            moves["qf", h, 2, s].wait_recv()
    last = [(2, 2)]
    finish(last)
    add(knight, 1)
    add(last, 0)
    add(last, 1)

    for n in range(NG - 1):
        for c in range(CAP):
            d_copy(n, c, False).wait_send()
        c_copy(n, False).wait_send()
    z_wait_send(cfull, 0)
    z_wait_send(cown, 3)
    z_wait_send(wz, 6)
    for copy in moves.values():
        copy.wait_send()


def local(colloc, potent, weights, density, list_owner, list_local):
    me = lax.axis_index("grid")
    part = lax.axis_index("ao")
    tab, keep = plan(list_owner, list_local, me, part)
    smem = pl.BlockSpec(memory_space=pltpu.SMEM)
    vmem = pl.BlockSpec(memory_space=pltpu.VMEM)
    dma = pltpu.SemaphoreType.DMA
    return pl.pallas_call(
        kernel,
        out_shape=jax.ShapeDtypeStruct((2 * RBS, TILES * RBS), F32),
        in_specs=[smem, smem, vmem, vmem, vmem, vmem],
        out_specs=vmem,
        scratch_shapes=[
            pltpu.VMEM((2 * N_COL, RBS, RBS), BF16),
            pltpu.VMEM((NG * CAP, RBS, 2 * RBS), BF16),
            pltpu.VMEM((NG * CAP, RBS, 2 * RBS), BF16),
            pltpu.VMEM((NA * 2 * BLK, RBS, RBS), BF16),
            pltpu.VMEM((NG, CAP, RBS // NA, RBS), BF16),
            pltpu.VMEM((NA * NG, CAP, RBS // NA, RBS), BF16),
            pltpu.VMEM((NA * 2 * BLK, RBS, RBS), BF16),
            pltpu.VMEM((NG, 2 * RBS, CAP * RBS), BF16),
            pltpu.VMEM((RBS, RBS), BF16),
        ]
        + [pltpu.VMEM((TILES + 1, RBS, RBS), BF16)] * NG
        + [
            dma((NG * CAP,)),
            dma((NG * CAP,)),
            dma((NG,)),
            dma((NG,)),
            dma((9,)),
            dma((9,)),
            dma((80,)),
            dma((80,)),
        ],
        compiler_params=pltpu.CompilerParams(
            collective_id=0, has_side_effects=True, vmem_limit_bytes=56 << 20
        ),
    )(tab, keep, colloc, potent, weights, density)


def solution(mesh):
    placed = (
        P("grid", None, "ao"),
        P("grid", None, "ao"),
        P("grid", None),
        P("grid", None),
        P(),
        P(),
    )
    return jax.shard_map(
        local, mesh=mesh, in_specs=placed, out_specs=P("grid", "ao"), check_vma=False
    )
```

time: 386 us -> 159 us (0.41)
  waiting for transfers between devices: 233 us -> 0 us
  Pallas kernels: 0 us -> 146 us
  local copies, waits for them, and re-layouts: 82 us -> 8.15 us
  other arithmetic: 34.1 us -> 2.37 us
  starting transfers between devices: 17 us -> 0 us
  between operations: 13.6 us -> 0.16 us
  matrix products: 5.01 us -> 0 us
    all_to_all x2 -> x0, waiting for transfers between devices: 148 us -> none  [the longest x1 99.6 us: local(): lax.all_to_all(sending, 'grid', split_axis=0, concat_axis=0, tiled=True)]
    pallas_call x0 -> x1, Pallas kernels: none -> 146 us  [local(): pl.pallas_call(kernel, out_shape=jax.ShapeDtypeStruct((2 * RBS, TILES * R...]
    reduce_scatter x1 -> x0, waiting for transfers between devices: 84.7 us -> none  [local(): return lax.psum_scatter(flat, 'ao', scatter_dimension=1, tiled=True)]
    scatter-add x1 -> x0, other arithmetic: 27 us -> none  [local(): totals = totals.at[row_local[:, :, None], :, col_blocks, :].add(pieces)]
    all_to_all x2 -> x0, starting transfers between devices: 16.9 us -> none  [the longest x1 8.78 us: local(): lax.all_to_all(outgoing, 'grid', split_axis=0, concat_axis=0, tiled=True)]
    gather x10 -> x0, local copies, waits for them, and re-layouts: 11.6 us -> none  [the longest x1 5.28 us: local(): tiles = blocked[row_local[:, :, None], :, col_blocks, :]]
    unnamed x11 -> x3, local copies, waits for them, and re-layouts: 15.3 us -> 4.72 us
    transpose x1 -> x0, local copies, waits for them, and re-layouts: 9 us -> none  [local(): jnp.transpose(incoming.reshape(n_grid, capacity, RBS, per_part, RBS), (0,...]
  transfers between devices with their start and end apart: 4 -> 0, of which waited for: 3 -> 0; matrix products, arithmetic and copies ran while one was open for 1% -> 0% of each run, Pallas kernels for 0% -> 0%
where the time goes in v1:
time: 159 us; the launch traced here: 157 us
  Pallas kernels  146 us (92%)
  local copies, waits for them, and re-layouts  8.15 us (5%)
  other arithmetic  2.37 us (1%)
    pallas_call x1, Pallas kernels, local(): pl.pallas_call(kernel, out_shape=jax.ShapeDtypeStruct((2 * RBS, TILES * R...  146 us
    unnamed x3, local copies, waits for them, and re-layouts  4.72 us

profile of v1, /device:TPU:1, one launch (start us, length us, event | category | flops | bytes accessed | tf_op | source)
XLA Modules:
  0.0 157.1 jit_solution(5869514996231662846)
XLA Ops:
  0.0 0.7 convert_reduce_fusion.1
  0.7 0.1 mul.230
  0.9 0.1 multiply_reduce_fusion.5
  1.0 0.1 mul.237
  1.2 0.1 copy.32
  1.3 0.1 copy.21
  1.4 0.1 mul.241
  1.5 0.1 copy.33
  1.6 0.1 fusion
  1.8 0.7 convert_element_type.54.keep
  2.4 0.8 copy.22
  3.2 0.1 mul.250
  3.3 0.1 convert_reduce_fusion
  3.4 0.1 multiply_reduce_fusion.3
  3.5 0.2 select_reduce_fusion.1
  3.7 0.1 reduce_sum.156
  3.8 0.1 copy.27
  3.9 0.1 reshape.203
  4.1 0.6 multiply_reduce_fusion
  4.9 0.1 multiply_reduce_fusion.2
  5.0 0.8 copy.23
  5.9 0.1 constant_dynamic-slice_fusion.2
  6.0 0.1 copy.24
  6.1 0.1 select_reduce_fusion
  6.3 0.1 copy.26
  6.4 0.1 squeeze.12
  6.5 0.1 copy.25
  6.5 0.1 squeeze.11
  6.8 0.1 add.138
  6.9 0.7 concatenate.3.tab
  7.5 146.4 %shard_map.64 = f32[256,2048]{1,0:T(8,128)} custom-call(s32[1264]{0:T(1024)} %concatenate.3.tab, f32[128]{0:T(128)} %convert_element_type.54.keep, bf16[4,128,256]{2,1,0:T(8,128)(2,1)} %colloc.1, bf16[4,128,256]{2,1,0:T(8,128)(2,1)} %potent.1, f32[4,128]{1,0:T(4,128)} %weights.1, bf16[256,8192]{1,0:T(8,128)(2,1)} %dens.1), custom_call_target="tpu_custom_call" | custom-call | tf_op jit(solution)/shard_map/pallas_call | solution.py:392
  154.0 3.1 %copy.35 = f32[256,2048]{1,0:T(8,128)} copy(f32[256,2048]{1,0:T(8,128)} %shard_map.64) | data formatting | bytes 4194304
  (25 shorter events, 0.7 us)

commit v2 on v1

--- a/solution.py
+++ b/solution.py
@@ -74,7 +74,7 @@
     my_rank = lax.dynamic_index_in_dim(rank, me, 0, keepdims=False)
     flat = jnp.arange(n, dtype=i32)
     b_of, k_of = flat // SIG, flat % SIG
-    stored = (k_of // 2) * (2 * BLK) + b_of * 2 + k_of % 2
+    stored = (k_of // 2) * (2 * BLK) + (k_of % 2) * BLK + b_of
     tiles = jnp.arange(TILES, dtype=i32)
     sel = jnp.sum(my_group[None] * (my_rank[None] == tiles[:, None]).astype(i32) * stored[None], axis=1)
 
@@ -95,7 +95,7 @@
     return tab, keep.reshape(-1)
 
 
-def kernel(tab, keep, colloc, potent, weights, dens, out, dtiles, send, arrived, cfull, cqs, cown, wz, lhs_t, picked, *rest):
+def kernel(tab, keep, colloc, potent, weights, dens, out, dtiles, send0, send1, arrived0, arrived1, cfull, cqs, cown, wz, lhs_t, picked, scaled, *rest):
     held = rest[: NG]
     dsend, drecv, csend, crecv, zsend, zrecv, gsend, grecv = rest[NG:]
     me = lax.axis_index("grid")
@@ -113,54 +113,60 @@
     for o in range(1, NA):
         pl.semaphore_signal(barrier, inc=1, device_id=(me, (part + o) % NA), device_id_type=MESH)
 
-    def pack(d, carry):
-        for c in range(CAP):
-            i = d * CAP + c
-            for h, base in enumerate((T_K0, T_K1)):
-                send[i, :, h * RBS : (h + 1) * RBS] = dtiles[tab[base + i]]
-        return carry
+    send = (send0, send1)
+    arrived = (arrived0, arrived1)
+
+    def pack(h):
+        def step(d, carry):
+            for c in range(CAP):
+                send[h][d * CAP + c] = dtiles[tab[(T_K0, T_K1)[h] + d * CAP + c]]
+            return carry
+
+        lax.fori_loop(0, NG, step, 0)
 
     for r in range(2):
         for k in range(N_COL):
             dtiles[r * N_COL + k] = dens[r * RBS : (r + 1) * RBS, k * RBS : (k + 1) * RBS]
-    lax.fori_loop(0, NG, pack, 0)
+    pack(0)
     for b in range(BLK):
         for h in range(2):
             cfull[part * 2 * BLK + 2 * b + h] = colloc[b, :, h * RBS : (h + 1) * RBS]
     pl.semaphore_wait(barrier, len(OFFSETS) + NA - 1)
 
-    def z_copy(buf, base, o, there):
-        count = buf.shape[0] // NA
+    def z_copy(buf, base, o, there, cut=(0, 1)):
+        whole = buf.shape[0] // NA
+        count = whole // cut[1]
+        low = cut[0] * count
         return pltpu.make_async_remote_copy(
-            src_ref=buf.at[pl.ds(part * count, count)],
-            dst_ref=buf.at[pl.ds(there * count, count)],
+            src_ref=buf.at[pl.ds(part * whole + low, count)],
+            dst_ref=buf.at[pl.ds(there * whole + low, count)],
             send_sem=zsend.at[base + o - 1],
             recv_sem=zrecv.at[base + o - 1],
             device_id=(me, (part + o) % NA),
             device_id_type=MESH,
         )
 
-    def z_start(buf, base):
+    def z_start(buf, base, cut=(0, 1)):
         for o in (2, 1, 3):
-            z_copy(buf, base, o, part).start()
-
-    def z_wait_recv(buf, base):
+            z_copy(buf, base, o, part, cut).start()
+
+    def z_wait_recv(buf, base, cut=(0, 1)):
         for o in (1, 3, 2):
-            z_copy(buf, base, o, (part + NA - o) % NA).wait_recv()
-
-    def z_wait_send(buf, base):
+            z_copy(buf, base, o, (part + NA - o) % NA, cut).wait_recv()
+
+    def z_wait_send(buf, base, cut=(0, 1)):
         for o in (1, 2, 3):
-            z_copy(buf, base, o, part).wait_send()
-
-    def d_copy(n, c, recv):
+            z_copy(buf, base, o, part, cut).wait_send()
+
+    def d_copy(n, h, recv):
         oy, ox, oc = OFFSETS[n]
         to = at_offset(oy, ox, oc)
         frm = at_offset(-oy, -ox, oc) if recv else me
         return pltpu.make_async_remote_copy(
-            src_ref=send.at[to * CAP + c],
-            dst_ref=arrived.at[frm * CAP + c],
-            send_sem=dsend.at[n * CAP + c],
-            recv_sem=drecv.at[n * CAP + c],
+            src_ref=send[h].at[pl.ds(to * CAP, CAP)],
+            dst_ref=arrived[h].at[pl.ds(frm * CAP, CAP)],
+            send_sem=dsend.at[n * 2 + h],
+            recv_sem=drecv.at[n * 2 + h],
             device_id=(to, part),
             device_id_type=MESH,
         )
@@ -181,8 +187,19 @@
     z_start(cfull, 0)
     for n in range(NG - 1):
         d_copy(n, 0, False).start()
-    for c in range(CAP):
-        arrived[me * CAP + c] = send[me * CAP + c]
+    pack(1)
+    for n in range(NG - 1):
+        d_copy(n, 1, False).start()
+    for h in range(2):
+        for c in range(CAP):
+            arrived[h][me * CAP + c] = send[h][me * CAP + c]
+    for b in range(BLK):
+        w = jnp.transpose(jnp.broadcast_to(weights[b : b + 1, :], (RBS, RBS)))
+        for h in range(2):
+            scaled[h * BLK + b] = w * potent[b, :, h * RBS : (h + 1) * RBS].astype(F32)
+    for s in range(NG):
+        held[s][TILES] = jnp.zeros((RBS, RBS), BF16)
+    out[...] = jnp.zeros_like(out)
 
     z_wait_recv(cfull, 0)
     quarter = RBS // NA
@@ -197,29 +214,22 @@
     lax.fori_loop(0, NG, pack_c, 0)
     for n in range(NG - 1):
         c_copy(n, False).start()
-    for n in range(NG - 1):
-        d_copy(n, 1, False).start()
     cown[part * NG + me] = cqs[me]
-    for s in range(NG):
-        held[s][TILES] = jnp.zeros((RBS, RBS), BF16)
+
+    for h in range(2):
+        for n in range(NG - 1):
+            d_copy(n, h, True).wait_recv()
+        for b in range(BLK):
+            left = jnp.concatenate([cfull[q * 2 * BLK + 2 * b + g] for q in range(NA) for g in range(2)], axis=1)
+            right = jnp.concatenate([arrived[h][tab[T_ARR + b * SIG + j]] for j in range(SIG)], axis=0)
+            f_vals = jnp.dot(left, right, preferred_element_type=F32)
+            wz[part * 2 * BLK + h * BLK + b] = (scaled[h * BLK + b] * f_vals).astype(BF16)
+        z_start(wz, 3 + 3 * h, (h, 2))
     for n in range(NG - 1):
         c_copy(n, True).wait_recv()
-    z_start(cown, 3)
-    for c in range(CAP):
-        for n in range(NG - 1):
-            d_copy(n, c, True).wait_recv()
-
-    for b in range(BLK):
-        left = jnp.concatenate([cfull[q * 2 * BLK + 2 * b + h] for q in range(NA) for h in range(2)], axis=1)
-        right = jnp.concatenate([arrived[tab[T_ARR + b * SIG + j]] for j in range(SIG)], axis=0)
-        f_vals = jnp.dot(left, right, preferred_element_type=F32)
-        w = jnp.transpose(jnp.broadcast_to(weights[b : b + 1, :], (RBS, RBS)))
-        for h in range(2):
-            cut = slice(h * RBS, (h + 1) * RBS)
-            wz[part * 2 * BLK + 2 * b + h] = (w * potent[b, :, cut].astype(F32) * f_vals[:, cut]).astype(BF16)
-    z_start(wz, 6)
-
-    z_wait_recv(cown, 3)
+    z_start(cown, 9)
+    for h in range(2):
+        z_wait_recv(wz, 3 + 3 * h, (h, 2))
 
     def build(d, carry):
         for c in range(CAP):
@@ -230,10 +240,6 @@
                     tile * keep[(d * CAP + c) * 2 + r]
                 ).astype(BF16)
         return carry
-
-    lax.fori_loop(0, NG, build, 0)
-    out[...] = jnp.zeros_like(out)
-    z_wait_recv(wz, 6)
 
     def piece(oy, ox, oc=0):
         return held[((oy % NY) * NX + ox % NX) * 2 + oc]
@@ -291,19 +297,11 @@
     def add_piece(oy, ox, oc):
         src = at_offset(-oy, -ox, oc)
         buf = piece(oy, ox, oc)
-        width = 4
-
-        def step(m, carry):
-            tiles = []
-            for c in range(CAP):
-                base = T_IDX + (src * CAP + c) * TILES + m * width
-                tiles.append(jnp.concatenate([buf[tab[base + w]] for w in range(width)], axis=1))
-            right = jnp.concatenate(tiles, axis=0)
-            cols = pl.ds(pl.multiple_of(m * width * RBS, width * RBS), width * RBS)
-            out[:, cols] += jnp.dot(lhs_t[src], right, preferred_element_type=F32)
-            return carry
-
-        lax.fori_loop(0, TILES // width, step, 0)
+        tiles = []
+        for c in range(CAP):
+            base = T_IDX + (src * CAP + c) * TILES
+            tiles.append(jnp.concatenate([buf[tab[base + w]] for w in range(TILES)], axis=1))
+        out[...] += jnp.dot(lhs_t[src], jnp.concatenate(tiles, axis=0), preferred_element_type=F32)
 
     def finish(pieces):
         for oy, ox in pieces:
@@ -320,7 +318,6 @@
     for h in range(2):
         send_second(h, 0)
     to_sibling(0, 0)
-    add([(0, 0)], 0)
     for s in (1, -1):
         for h in range(2):
             forward_first(h, s)
@@ -334,8 +331,6 @@
         for s in (1, -1):
             moves["pf", h, s].wait_recv()
         send_second(h, 2)
-    add([(0, 0)], 1)
-    add(near, 0)
     diagonal = [(1, 1), (1, -1), (-1, 1), (-1, -1)]
     for i in (1, -1):
         for s in (1, -1):
@@ -347,20 +342,20 @@
             moves["qf", h, 0, s].wait_recv()
     straight = [(0, 2), (2, 0)]
     finish(straight)
-    add(near, 1)
-    add(diagonal, 0)
     for s in (1, -1):
         for h in range(2):
             forward_second(h, 2, s)
-    add(straight, 0)
-    add(diagonal, 1)
+    z_wait_recv(cown, 9)
+    lax.fori_loop(0, NG, build, 0)
+    for pieces in ([(0, 0)], near, diagonal, straight):
+        add(pieces, 0)
+        add(pieces, 1)
     for i in (1, -1):
         for h in range(2):
             for s in (1, -1):
                 moves["qf", h, i, s].wait_recv()
     knight = [(1, 2), (-1, 2), (2, 1), (2, -1)]
     finish(knight)
-    add(straight, 1)
     add(knight, 0)
     for h in range(2):
         for s in (1, -1):
@@ -372,12 +367,13 @@
     add(last, 1)
 
     for n in range(NG - 1):
-        for c in range(CAP):
-            d_copy(n, c, False).wait_send()
+        for h in range(2):
+            d_copy(n, h, False).wait_send()
         c_copy(n, False).wait_send()
     z_wait_send(cfull, 0)
-    z_wait_send(cown, 3)
-    z_wait_send(wz, 6)
+    for h in range(2):
+        z_wait_send(wz, 3 + 3 * h, (h, 2))
+    z_wait_send(cown, 9)
     for copy in moves.values():
         copy.wait_send()
 
@@ -396,23 +392,26 @@
         out_specs=vmem,
         scratch_shapes=[
             pltpu.VMEM((2 * N_COL, RBS, RBS), BF16),
-            pltpu.VMEM((NG * CAP, RBS, 2 * RBS), BF16),
-            pltpu.VMEM((NG * CAP, RBS, 2 * RBS), BF16),
+            pltpu.VMEM((NG * CAP, RBS, RBS), BF16),
+            pltpu.VMEM((NG * CAP, RBS, RBS), BF16),
+            pltpu.VMEM((NG * CAP, RBS, RBS), BF16),
+            pltpu.VMEM((NG * CAP, RBS, RBS), BF16),
             pltpu.VMEM((NA * 2 * BLK, RBS, RBS), BF16),
             pltpu.VMEM((NG, CAP, RBS // NA, RBS), BF16),
             pltpu.VMEM((NA * NG, CAP, RBS // NA, RBS), BF16),
             pltpu.VMEM((NA * 2 * BLK, RBS, RBS), BF16),
             pltpu.VMEM((NG, 2 * RBS, CAP * RBS), BF16),
             pltpu.VMEM((RBS, RBS), BF16),
+            pltpu.VMEM((2 * BLK, RBS, RBS), F32),
         ]
         + [pltpu.VMEM((TILES + 1, RBS, RBS), BF16)] * NG
         + [
-            dma((NG * CAP,)),
-            dma((NG * CAP,)),
+            dma((NG * 2,)),
+            dma((NG * 2,)),
             dma((NG,)),
             dma((NG,)),
-            dma((9,)),
-            dma((9,)),
+            dma((12,)),
+            dma((12,)),
             dma((80,)),
             dma((80,)),
         ],

time: 159 us -> 146 us (0.918)
  Pallas kernels: 146 us -> 134 us
    pallas_call x1, Pallas kernels: 146 us -> 134 us  [local(): pl.pallas_call(kernel, out_shape=jax.ShapeDtypeStruct((2 * RBS, TILES * R...]
where the time goes in v2:
time: 146 us; the launch traced here: 145 us
  Pallas kernels  134 us (92%)
  local copies, waits for them, and re-layouts  8.15 us (6%)
  other arithmetic  2.37 us (2%)
    pallas_call x1, Pallas kernels, local(): pl.pallas_call(kernel, out_shape=jax.ShapeDtypeStruct((2 * RBS, TILES * R...  134 us
    unnamed x3, local copies, waits for them, and re-layouts  4.72 us

profile of v2, /device:TPU:1, one launch (start us, length us, event | category | flops | bytes accessed | tf_op | source)
XLA Modules:
  0.0 145.0 jit_solution(12937182408508379684)
XLA Ops:
  0.0 0.7 convert_reduce_fusion.1
  0.7 0.1 mul.232
  0.9 0.1 multiply_reduce_fusion.5
  1.0 0.1 mul.239
  1.2 0.1 copy.32
  1.3 0.1 copy.21
  1.4 0.1 mul.243
  1.5 0.1 copy.33
  1.6 0.1 fusion
  1.8 0.7 convert_element_type.54.keep
  2.4 0.8 copy.22
  3.2 0.1 mul.252
  3.3 0.1 convert_reduce_fusion
  3.4 0.1 multiply_reduce_fusion.3
  3.5 0.2 select_reduce_fusion.1
  3.7 0.1 reduce_sum.156
  3.8 0.1 copy.27
  3.9 0.1 reshape.203
  4.1 0.6 multiply_reduce_fusion
  4.9 0.1 multiply_reduce_fusion.2
  5.0 0.8 copy.23
  5.9 0.1 constant_dynamic-slice_fusion.2
  6.0 0.1 copy.24
  6.1 0.1 select_reduce_fusion
  6.3 0.1 copy.26
  6.4 0.1 squeeze.12
  6.5 0.1 copy.25
  6.5 0.1 squeeze.11
  6.8 0.1 add.138
  6.9 0.7 concatenate.3.tab
  7.5 134.3 %shard_map.64 = f32[256,2048]{1,0:T(8,128)} custom-call(s32[1264]{0:T(1024)} %concatenate.3.tab, f32[128]{0:T(128)} %convert_element_type.54.keep, bf16[4,128,256]{2,1,0:T(8,128)(2,1)} %colloc.1, bf16[4,128,256]{2,1,0:T(8,128)(2,1)} %potent.1, f32[4,128]{1,0:T(4,128)} %weights.1, bf16[256,8192]{1,0:T(8,128)(2,1)} %dens.1), custom_call_target="tpu_custom_call" | custom-call | tf_op jit(solution)/shard_map/pallas_call | solution.py:388
  141.8 3.1 %copy.35 = f32[256,2048]{1,0:T(8,128)} copy(f32[256,2048]{1,0:T(8,128)} %shard_map.64) | data formatting | bytes 4194304
  (25 shorter events, 0.7 us)

commit v3 on v2

v3 whole, which is shorter than its diff:
```python
import functools

import jax
import jax.numpy as jnp
from jax import lax
from jax.experimental import pallas as pl
from jax.experimental.pallas import tpu as pltpu
from jax.sharding import PartitionSpec as P

RBS = 128
SIG = 8
BLK = 4
NG = 32
NA = 4
NY = 4
NX = 4
CAP = 2
TILES = 16
FEW = 13
N_COL = 64
MESH = pl.DeviceIdType.MESH
F32 = jnp.float32
BF16 = jnp.bfloat16

LANES = 128
T_ARR = 0
T_DENS = T_ARR + SIG
T_CB = T_DENS + 2 * CAP
T_SEL = T_CB + 1
T_IDX = 16
T_END = T_IDX + CAP * TILES


def exchange_order():
    far = sorted(
        [(oy, ox, oc) for oy in range(NY) for ox in range(NX) for oc in range(2) if (oy, ox, oc) != (0, 0, 0)],
        key=lambda o: -(min(o[0], NY - o[0]) + min(o[1], NX - o[1])),
    )
    order = []
    for first in far:
        turned = first
        for _ in range(4):
            if turned not in order:
                order.append(turned)
            turned = (turned[1] % NY, -turned[0] % NX, turned[2])
    return order


OFFSETS = exchange_order()


def plan_kernel(own_ref, loc_ref, tab, keep, few):
    me = lax.axis_index("grid")
    part = lax.axis_index("ao")
    i32 = jnp.int32
    own = own_ref[...]
    loc = loc_ref[...]
    shape = (SIG, LANES)
    slot = lax.broadcasted_iota(i32, shape, 0)
    lane = lax.broadcasted_iota(i32, shape, 1)
    block = lane % BLK
    row1 = (1, LANES)
    block1 = lax.broadcasted_iota(i32, row1, 1) % BLK
    row_ids = own * 2 + loc

    def total(v):
        return jnp.sum(v, axis=0, keepdims=True)

    def earlier(v, blk):
        out = jnp.zeros_like(v)
        for s in range(1, BLK):
            out += jnp.where(blk >= s, pltpu.roll(v, s, 1), 0)
        return out

    def over_blocks(v):
        out = v
        for s in range(1, BLK):
            out += pltpu.roll(v, LANES - s, 1)
        return out

    hit = (own == me).astype(i32)
    named = total(hit)
    before = earlier(named, block1)
    row = total(hit * loc)
    cols = [total(jnp.where(slot == part * 2 + h, row_ids, 0)) for h in range(2)]
    chosen = [named * (before == c).astype(i32) for c in range(CAP)]
    for c in range(CAP):
        for h in range(2):
            tab[T_DENS + h * CAP + c, :] = over_blocks(chosen[c] * (row * N_COL + cols[h]))[0]
        for r in range(2):
            keep[c * 2 + r, :] = over_blocks(chosen[c] * (row == r).astype(i32))[0].astype(F32)

    spot = jnp.zeros(shape, i32)
    for s in range(1, BLK):
        prior = pltpu.roll(own, s, 1)
        for j in range(SIG):
            turned = prior if j == 0 else pltpu.roll(prior, j, 0)
            spot += jnp.where((block >= s) & (turned == own), 1, 0)
    arr = own * CAP + spot
    tab[T_ARR : T_ARR + SIG, :] = arr

    group = (own // (NG // NA) == part).astype(i32)
    rank = earlier(total(group), block1) + jnp.zeros(shape, i32)
    for s in range(1, SIG):
        rank += jnp.where(slot >= s, pltpu.roll(group, s, 0), 0)
    to_me = LANES - me * BLK
    my_arr = pltpu.roll(arr, to_me, 1)
    my_rank = pltpu.roll(jnp.where(group > 0, rank, LANES), to_me, 1)
    cb = jnp.zeros(row1, i32)
    sel = jnp.zeros(row1, i32)
    for b in range(BLK):
        at = (slot // 2) * (2 * BLK) + 2 * b + slot % 2
        cb += total(jnp.where(jnp.broadcast_to(my_arr[:, b : b + 1], shape) == lane, at, 0))
        at = (slot // 2) * (2 * BLK) + (slot % 2) * BLK + b
        sel += total(jnp.where(jnp.broadcast_to(my_rank[:, b : b + 1], shape) == lane, at, 0))
    tab[T_CB, :] = cb[0]
    tab[T_SEL, :] = sel[0]
    for n in range(TILES):
        at = total(jnp.where(row_ids == part * TILES + n, rank + 1, 0))
        for c in range(CAP):
            tab[T_IDX + c * TILES + n, :] = over_blocks(chosen[c] * at)[0]

    most = jnp.zeros(row1, i32)
    for z in range(NA):
        most = jnp.maximum(most, over_blocks(total((own // (NG // NA) == z).astype(i32))))
    most = jnp.where(block1 == 0, most, 0)
    few[0, 0] = (jnp.max(most) <= FEW).astype(i32)


def kernel(count, tab, keep, colloc, potent, weights, dens, out, dtiles, send0, send1, arrived0, arrived1, cfull, cqs, cown, wz, lhs_t, picked, scaled, dloc, *rest):
    held = rest[: NG]
    dsend, drecv, csend, crecv, zsend, zrecv, gsend, grecv, lsem = rest[NG:]
    me = lax.axis_index("grid")
    part = lax.axis_index("ao")
    y = me // (2 * NX)
    x = (me // 2) % NX
    core = me % 2

    def at_offset(oy, ox, oc):
        return ((y + oy + NY) % NY) * (2 * NX) + ((x + ox + NX) % NX) * 2 + (core + oc) % 2

    rows_in = [
        pltpu.make_async_copy(dens.at[pl.ds(r * RBS, RBS)], dloc.at[pl.ds(r * RBS, RBS)], lsem.at[r]) for r in range(2)
    ]
    for copy in rows_in:
        copy.start()
    barrier = pltpu.get_barrier_semaphore()
    for o in OFFSETS:
        pl.semaphore_signal(barrier, inc=1, device_id=(at_offset(*o), part), device_id_type=MESH)
    for o in range(1, NA):
        pl.semaphore_signal(barrier, inc=1, device_id=(me, (part + o) % NA), device_id_type=MESH)

    send = (send0, send1)
    arrived = (arrived0, arrived1)

    def pack(h):
        def step(d, carry):
            for c in range(CAP):
                send[h][d * CAP + c] = dtiles[tab[T_DENS + h * CAP + c, d * BLK]]
            return carry

        lax.fori_loop(0, NG, step, 0)

    for r in range(2):
        rows_in[r].wait()
        for k in range(N_COL):
            dtiles[r * N_COL + k] = dloc[r * RBS : (r + 1) * RBS, k * RBS : (k + 1) * RBS]
    pack(0)
    for b in range(BLK):
        for h in range(2):
            cfull[part * 2 * BLK + 2 * b + h] = colloc[b, :, h * RBS : (h + 1) * RBS]
    pl.semaphore_wait(barrier, len(OFFSETS) + NA - 1)

    def z_copy(buf, base, o, there, cut=(0, 1)):
        whole = buf.shape[0] // NA
        count = whole // cut[1]
        low = cut[0] * count
        return pltpu.make_async_remote_copy(
            src_ref=buf.at[pl.ds(part * whole + low, count)],
            dst_ref=buf.at[pl.ds(there * whole + low, count)],
            send_sem=zsend.at[base + o - 1],
            recv_sem=zrecv.at[base + o - 1],
            device_id=(me, (part + o) % NA),
            device_id_type=MESH,
        )

    def z_start(buf, base, cut=(0, 1)):
        for o in (2, 1, 3):
            z_copy(buf, base, o, part, cut).start()

    def z_wait_recv(buf, base, cut=(0, 1)):
        for o in (1, 3, 2):
            z_copy(buf, base, o, (part + NA - o) % NA, cut).wait_recv()

    def z_wait_send(buf, base, cut=(0, 1)):
        for o in (1, 2, 3):
            z_copy(buf, base, o, part, cut).wait_send()

    def d_copy(n, h, recv):
        oy, ox, oc = OFFSETS[n]
        to = at_offset(oy, ox, oc)
        frm = at_offset(-oy, -ox, oc) if recv else me
        return pltpu.make_async_remote_copy(
            src_ref=send[h].at[pl.ds(to * CAP, CAP)],
            dst_ref=arrived[h].at[pl.ds(frm * CAP, CAP)],
            send_sem=dsend.at[n * 2 + h],
            recv_sem=drecv.at[n * 2 + h],
            device_id=(to, part),
            device_id_type=MESH,
        )

    def c_copy(n, recv):
        oy, ox, oc = OFFSETS[n]
        to = at_offset(oy, ox, oc)
        frm = at_offset(-oy, -ox, oc) if recv else me
        return pltpu.make_async_remote_copy(
            src_ref=cqs.at[to],
            dst_ref=cown.at[part * NG + frm],
            send_sem=csend.at[n],
            recv_sem=crecv.at[n],
            device_id=(to, part),
            device_id_type=MESH,
        )

    z_start(cfull, 0)
    for n in range(NG - 1):
        d_copy(n, 0, False).start()
    pack(1)
    for n in range(NG - 1):
        d_copy(n, 1, False).start()
    for h in range(2):
        for c in range(CAP):
            arrived[h][me * CAP + c] = send[h][me * CAP + c]
    for b in range(BLK):
        w = jnp.transpose(jnp.broadcast_to(weights[b : b + 1, :], (RBS, RBS)))
        for h in range(2):
            scaled[h * BLK + b] = w * potent[b, :, h * RBS : (h + 1) * RBS].astype(F32)
    for s in range(NG):
        held[s][0] = jnp.zeros((RBS, RBS), BF16)
    out[...] = jnp.zeros_like(out)

    z_wait_recv(cfull, 0)
    quarter = RBS // NA

    def pack_c(o, carry):
        for c in range(CAP):
            picked[...] = cfull[tab[T_CB, o * CAP + c]]
            rows = pl.multiple_of(part * quarter, quarter)
            cqs[o, c] = picked[pl.ds(rows, quarter), :]
        return carry

    lax.fori_loop(0, NG, pack_c, 0)
    for n in range(NG - 1):
        c_copy(n, False).start()
    cown[part * NG + me] = cqs[me]

    for h in range(2):
        for n in range(NG - 1):
            d_copy(n, h, True).wait_recv()
        for b in range(BLK):
            left = jnp.concatenate([cfull[q * 2 * BLK + 2 * b + g] for q in range(NA) for g in range(2)], axis=1)
            right = jnp.concatenate([arrived[h][tab[T_ARR + j, me * BLK + b]] for j in range(SIG)], axis=0)
            f_vals = jnp.dot(left, right, preferred_element_type=F32)
            wz[part * 2 * BLK + h * BLK + b] = (scaled[h * BLK + b] * f_vals).astype(BF16)
        z_start(wz, 3 + 3 * h, (h, 2))
    for n in range(NG - 1):
        c_copy(n, True).wait_recv()
    z_start(cown, 9)
    for h in range(2):
        z_wait_recv(wz, 3 + 3 * h, (h, 2))

    def build(d, carry):
        for c in range(CAP):
            tile = jnp.concatenate([cown[q * NG + d, c].astype(F32) for q in range(NA)], axis=0)
            tile = jnp.transpose(tile)
            for r in range(2):
                lhs_t[d, r * RBS : (r + 1) * RBS, c * RBS : (c + 1) * RBS] = (
                    tile * keep[c * 2 + r, d * BLK]
                ).astype(BF16)
        return carry

    def piece(oy, ox, oc=0):
        return held[((oy % NY) * NX + ox % NX) * 2 + oc]

    own = piece(0, 0)
    for t in range(count):
        own[1 + t] = wz[tab[T_SEL, t]]

    moves = {}

    def move(key, oy, ox, low, size, dy, dx, dc=0):
        n = len(moves)
        rows = pl.ds(1 + low, size)
        copy = pltpu.make_async_remote_copy(
            src_ref=piece(oy, ox).at[rows],
            dst_ref=piece(oy + dy, ox + dx, dc).at[rows],
            send_sem=gsend.at[n],
            recv_sem=grecv.at[n],
            device_id=(at_offset(dy, dx, dc), part),
            device_id_type=MESH,
        )
        moves[key] = copy
        copy.start()

    first = ((0, 1), (1, 0))
    second = ((1, 0), (0, 1))
    sizes = (count - count // 2, count // 2)
    lows = (0, sizes[0])

    def along(h, i, s=0):
        (py, px), (qy, qx) = first[h], second[h]
        return (i * py + s * qy, i * px + s * qx)

    def send_first(h):
        for s in (1, -1):
            move(("p", h, s), 0, 0, lows[h], sizes[h], *along(h, s))

    def send_second(h, i):
        for s in (1, -1):
            move(("q", h, i, s), *along(h, i), lows[h], sizes[h], *along(h, 0, s))

    def split(h, s):
        near_half = sizes[h] // 2 if h else sizes[h] - sizes[h] // 2
        return (lows[h], near_half) if s > 0 else (lows[h] + near_half, sizes[h] - near_half)

    def forward_first(h, s):
        moves["p", h, s].wait_recv()
        move(("pf", h, s), *along(h, s), *split(h, s), *along(h, s))

    def forward_second(h, i, s):
        moves["q", h, i, s].wait_recv()
        move(("qf", h, i, s), *along(h, i, s), *split(h, s), *along(h, 0, s))

    def to_sibling(oy, ox):
        move(("s", oy % NY, ox % NX), oy, ox, 0, count, 0, 0, 1)

    def add_piece(oy, ox, oc):
        src = at_offset(-oy, -ox, oc)
        buf = piece(oy, ox, oc)
        tiles = []
        for c in range(CAP):
            base = T_IDX + c * TILES
            tiles.append(jnp.concatenate([buf[tab[base + w, src * BLK]] for w in range(TILES)], axis=1))
        out[...] += jnp.dot(lhs_t[src], jnp.concatenate(tiles, axis=0), preferred_element_type=F32)

    def finish(pieces):
        for oy, ox in pieces:
            to_sibling(oy, ox)

    def add(pieces, oc):
        for oy, ox in pieces:
            if oc:
                moves["s", oy % NY, ox % NX].wait_recv()
            add_piece(oy, ox, oc)

    for h in range(2):
        send_first(h)
    for h in range(2):
        send_second(h, 0)
    to_sibling(0, 0)
    for s in (1, -1):
        for h in range(2):
            forward_first(h, s)
            send_second(h, s)
    for s in (1, -1):
        for h in range(2):
            forward_second(h, 0, s)
    near = [(0, 1), (0, -1), (1, 0), (-1, 0)]
    finish(near)
    for h in range(2):
        for s in (1, -1):
            moves["pf", h, s].wait_recv()
        send_second(h, 2)
    diagonal = [(1, 1), (1, -1), (-1, 1), (-1, -1)]
    for i in (1, -1):
        for s in (1, -1):
            for h in range(2):
                forward_second(h, i, s)
    finish(diagonal)
    for h in range(2):
        for s in (1, -1):
            moves["qf", h, 0, s].wait_recv()
    straight = [(0, 2), (2, 0)]
    finish(straight)
    for s in (1, -1):
        for h in range(2):
            forward_second(h, 2, s)
    z_wait_recv(cown, 9)
    lax.fori_loop(0, NG, build, 0)
    for pieces in ([(0, 0)], near, diagonal, straight):
        add(pieces, 0)
        add(pieces, 1)
    for i in (1, -1):
        for h in range(2):
            for s in (1, -1):
                moves["qf", h, i, s].wait_recv()
    knight = [(1, 2), (-1, 2), (2, 1), (2, -1)]
    finish(knight)
    for n in range(NG - 1):
        for h in range(2):
            d_copy(n, h, False).wait_send()
        c_copy(n, False).wait_send()
    z_wait_send(cfull, 0)
    for h in range(2):
        z_wait_send(wz, 3 + 3 * h, (h, 2))
    z_wait_send(cown, 9)
    add(knight, 0)
    add(knight, 1)
    earlier = list(moves.values())
    for h in range(2):
        for s in (1, -1):
            moves["qf", h, 2, s].wait_recv()
        move(("s2", h), 2, 2, lows[h], sizes[h], 0, 0, 1)
    add_piece(2, 2, 0)
    for copy in earlier:
        copy.wait_send()
    for h in range(2):
        moves["s2", h].wait_recv()
    add_piece(2, 2, 1)
    for h in range(2):
        moves["s2", h].wait_send()


def local(colloc, potent, weights, density, list_owner, list_local):
    smem = pl.BlockSpec(memory_space=pltpu.SMEM)
    vmem = pl.BlockSpec(memory_space=pltpu.VMEM)
    tab, keep, few = pl.pallas_call(
        plan_kernel,
        out_shape=(
            jax.ShapeDtypeStruct((T_END, LANES), jnp.int32),
            jax.ShapeDtypeStruct((2 * CAP, LANES), F32),
            jax.ShapeDtypeStruct((1, 1), jnp.int32),
        ),
        in_specs=[vmem, vmem],
        out_specs=(vmem, vmem, smem),
    )(list_owner.T, list_local.T)
    dma = pltpu.SemaphoreType.DMA
    def exchange(count, collective_id):
        return pl.pallas_call(
            functools.partial(kernel, count),
            out_shape=pltpu.VMEM((2 * RBS, TILES * RBS), F32),
            in_specs=[smem, smem, vmem, vmem, vmem, pl.BlockSpec(memory_space=pl.ANY)],
            out_specs=vmem,
            scratch_shapes=[
                pltpu.VMEM((2 * N_COL, RBS, RBS), BF16),
                pltpu.VMEM((NG * CAP, RBS, RBS), BF16),
                pltpu.VMEM((NG * CAP, RBS, RBS), BF16),
                pltpu.VMEM((NG * CAP, RBS, RBS), BF16),
                pltpu.VMEM((NG * CAP, RBS, RBS), BF16),
                pltpu.VMEM((NA * 2 * BLK, RBS, RBS), BF16),
                pltpu.VMEM((NG, CAP, RBS // NA, RBS), BF16),
                pltpu.VMEM((NA * NG, CAP, RBS // NA, RBS), BF16),
                pltpu.VMEM((NA * 2 * BLK, RBS, RBS), BF16),
                pltpu.VMEM((NG, 2 * RBS, CAP * RBS), BF16),
                pltpu.VMEM((RBS, RBS), BF16),
                pltpu.VMEM((2 * BLK, RBS, RBS), F32),
                pltpu.VMEM((2 * RBS, N_COL * RBS), BF16),
            ]
            + [pltpu.VMEM((count + 1, RBS, RBS), BF16)] * NG
            + [
                dma((NG * 2,)),
                dma((NG * 2,)),
                dma((NG,)),
                dma((NG,)),
                dma((12,)),
                dma((12,)),
                dma((80,)),
                dma((80,)),
                dma((2,)),
            ],
            compiler_params=pltpu.CompilerParams(
                collective_id=collective_id, has_side_effects=True, vmem_limit_bytes=56 << 20
            ),
        )

    return lax.cond(
        few[0, 0] > 0,
        exchange(FEW, 0),
        exchange(TILES, 1),
        tab, keep, colloc, potent, weights, density,
    )


def solution(mesh):
    placed = (
        P("grid", None, "ao"),
        P("grid", None, "ao"),
        P("grid", None),
        P("grid", None),
        P(),
        P(),
    )
    return jax.shard_map(
        local, mesh=mesh, in_specs=placed, out_specs=P("grid", "ao"), check_vma=False
    )
```

time: 146 us -> 127 us (0.87)
  Pallas kernels: 134 us -> 124 us
  local copies, waits for them, and re-layouts: 8.15 us -> 1.32 us
  other arithmetic: 2.37 us -> 0 us
    pallas_call x1 -> x2, Pallas kernels: 134 us -> 124 us  [the longest x1 123 us: local(): lax.cond(few[0, 0] > 0, exchange(FEW, 0), exchange(TILES, 1), tab, keep,...]
    unnamed x3 -> x1, local copies, waits for them, and re-layouts: 4.72 us -> 1.32 us
    reduce_sum x12 -> x0, other arithmetic: 2.13 us -> none  [the longest x1 0.72 us: plan(): named = jnp.sum(hit, axis=2)]
where the time goes in v3:
time: 127 us
  Pallas kernels  124 us (98%)
  local copies, waits for them, and re-layouts  1.32 us (1%)
    pallas_call x1, Pallas kernels, local(): lax.cond(few[0, 0] > 0, exchange(FEW, 0), exchange(TILES, 1), tab, keep,...  123 us

profile of v3, /device:TPU:1, one launch (start us, length us, event | category | flops | bytes accessed | tf_op | source)
XLA Modules:
  0.0 126.6 jit_solution(12503598744661344898)
XLA Ops:
  0.0 1.6 %shard_map.66 = (s32[48,128]{1,0:T(8,128)S(1)}, f32[4,128]{1,0:T(4,128)S(1)}, s32[1,1]{1,0:T(1,128)}) custom-call(s32[8,128]{1,0:T(8,128)} %bitcast.3, s32[8,128]{1,0:T(8,128)} %bitcast.4), custom_call_target="tpu_custom_call" | custom-call | tf_op jit(solution)/shard_map/pallas_call | solution.py:427
  2.2 123.0 %conditional.1 = (f32[256,2048]{1,0:T(8,128)S(1)}) conditional(s32[]{:T(128)} %bitcast.2, (s32[48,128]{1,0:T(8,128)S(1)}, f32[4,128]{1,0:T(4,128)S(1)}, bf16[4,128,256]{2,1,0:T(8,128)(2,1)}, bf16[4,128,256]{2,1,0:T(8,128)(2,1)}, f32[4,128]{1,0:T(4,128)}, /*index=5*/bf16[256,8192]{1,0:T(8,128)(2,1)}) %tuple.11, (s32[48,128]{1,0:T(8,128)S(1)}, ...), branch_computations={%region_0.0_spmd, %region_1.0_spmd} | conditional | bytes 8 | solution.py:476
  2.4 122.8 %branch_1_fun.1 = f32[256,2048]{1,0:T(8,128)S(1)} custom-call(s32[48,128]{1,0:T(8,128)S(1)} %get-tuple-element.38.tab, f32[4,128]{1,0:T(4,128)S(1)} %get-tuple-element.39.keep, bf16[4,128,256]{2,1,0:T(8,128)(2,1)} %get-tuple-element.40.colloc, bf16[4,128,256]{2,1,0:T(8,128)(2,1)} %get-tuple-element.41.potent, f32[4,128]{1,0:T(4,128)} %get-tuple-element.42.weights, ...), custom_call_target="tpu_custom_call" | custom-call | tf_op jit(solution)/shard_map/cond/branch_1_fun/pallas_call | solution.py:476
  125.3 1.3 %copy.12 = f32[256,2048]{1,0:T(8,128)} copy(f32[256,2048]{1,0:T(8,128)S(1)} %get-tuple-element.50) | data formatting | bytes 4194304

commit v4 on v3

--- a/solution.py
+++ b/solution.py
@@ -250,8 +250,6 @@
         return carry
 
     lax.fori_loop(0, NG, pack_c, 0)
-    for n in range(NG - 1):
-        c_copy(n, False).start()
     cown[part * NG + me] = cqs[me]
 
     for h in range(2):
@@ -262,12 +260,11 @@
             right = jnp.concatenate([arrived[h][tab[T_ARR + j, me * BLK + b]] for j in range(SIG)], axis=0)
             f_vals = jnp.dot(left, right, preferred_element_type=F32)
             wz[part * 2 * BLK + h * BLK + b] = (scaled[h * BLK + b] * f_vals).astype(BF16)
-        z_start(wz, 3 + 3 * h, (h, 2))
+        z_start(wz, 6 + 3 * h, (h, 2))
     for n in range(NG - 1):
-        c_copy(n, True).wait_recv()
-    z_start(cown, 9)
-    for h in range(2):
-        z_wait_recv(wz, 3 + 3 * h, (h, 2))
+        c_copy(n, False).start()
+    for h in range(2):
+        z_wait_recv(wz, 6 + 3 * h, (h, 2))
 
     def build(d, carry):
         for c in range(CAP):
@@ -358,6 +355,9 @@
     for h in range(2):
         send_second(h, 0)
     to_sibling(0, 0)
+    for n in range(NG - 1):
+        c_copy(n, True).wait_recv()
+    z_start(cown, 3)
     for s in (1, -1):
         for h in range(2):
             forward_first(h, s)
@@ -385,7 +385,7 @@
     for s in (1, -1):
         for h in range(2):
             forward_second(h, 2, s)
-    z_wait_recv(cown, 9)
+    z_wait_recv(cown, 3)
     lax.fori_loop(0, NG, build, 0)
     for pieces in ([(0, 0)], near, diagonal, straight):
         add(pieces, 0)
@@ -402,8 +402,8 @@
         c_copy(n, False).wait_send()
     z_wait_send(cfull, 0)
     for h in range(2):
-        z_wait_send(wz, 3 + 3 * h, (h, 2))
-    z_wait_send(cown, 9)
+        z_wait_send(wz, 6 + 3 * h, (h, 2))
+    z_wait_send(cown, 3)
     add(knight, 0)
     add(knight, 1)
     earlier = list(moves.values())
@@ -462,8 +462,8 @@
                 dma((NG * 2,)),
                 dma((NG,)),
                 dma((NG,)),
-                dma((12,)),
-                dma((12,)),
+                dma((6 + 6 * BLK,)),
+                dma((6 + 6 * BLK,)),
                 dma((80,)),
                 dma((80,)),
                 dma((2,)),

time: 127 us -> 121 us (0.953)
  Pallas kernels: 124 us -> 119 us
    pallas_call x1, Pallas kernels: 123 us -> 117 us  [local(): lax.cond(few[0, 0] > 0, exchange(FEW, 0), exchange(TILES, 1), tab, keep,...]
where the time goes in v4:
time: 121 us
  Pallas kernels  119 us (98%)
  local copies, waits for them, and re-layouts  1.32 us (1%)
    pallas_call x1, Pallas kernels, local(): lax.cond(few[0, 0] > 0, exchange(FEW, 0), exchange(TILES, 1), tab, keep,...  117 us

profile of v4, /device:TPU:1, one launch (start us, length us, event | category | flops | bytes accessed | tf_op | source)
XLA Modules:
  0.0 121.0 jit_solution(3497427061943464994)
XLA Ops:
  0.0 1.6 %shard_map.66 = (s32[48,128]{1,0:T(8,128)S(1)}, f32[4,128]{1,0:T(4,128)S(1)}, s32[1,1]{1,0:T(1,128)}) custom-call(s32[8,128]{1,0:T(8,128)} %bitcast.3, s32[8,128]{1,0:T(8,128)} %bitcast.4), custom_call_target="tpu_custom_call" | custom-call | tf_op jit(solution)/shard_map/pallas_call | solution.py:427
  2.2 117.4 %conditional.1 = (f32[256,2048]{1,0:T(8,128)S(1)}) conditional(s32[]{:T(128)} %bitcast.2, (s32[48,128]{1,0:T(8,128)S(1)}, f32[4,128]{1,0:T(4,128)S(1)}, bf16[4,128,256]{2,1,0:T(8,128)(2,1)}, bf16[4,128,256]{2,1,0:T(8,128)(2,1)}, f32[4,128]{1,0:T(4,128)}, /*index=5*/bf16[256,8192]{1,0:T(8,128)(2,1)}) %tuple.11, (s32[48,128]{1,0:T(8,128)S(1)}, ...), branch_computations={%region_0.0_spmd, %region_1.0_spmd} | conditional | bytes 8 | solution.py:476
  2.4 117.2 %branch_1_fun.1 = f32[256,2048]{1,0:T(8,128)S(1)} custom-call(s32[48,128]{1,0:T(8,128)S(1)} %get-tuple-element.38.tab, f32[4,128]{1,0:T(4,128)S(1)} %get-tuple-element.39.keep, bf16[4,128,256]{2,1,0:T(8,128)(2,1)} %get-tuple-element.40.colloc, bf16[4,128,256]{2,1,0:T(8,128)(2,1)} %get-tuple-element.41.potent, f32[4,128]{1,0:T(4,128)} %get-tuple-element.42.weights, ...), custom_call_target="tpu_custom_call" | custom-call | tf_op jit(solution)/shard_map/cond/branch_1_fun/pallas_call | solution.py:476
  119.6 1.3 %copy.12 = f32[256,2048]{1,0:T(8,128)} copy(f32[256,2048]{1,0:T(8,128)S(1)} %get-tuple-element.50) | data formatting | bytes 4194304

commit v5 on v4

--- a/solution.py
+++ b/solution.py
@@ -331,6 +331,9 @@
     def to_sibling(oy, ox):
         move(("s", oy % NY, ox % NX), oy, ox, 0, count, 0, 0, 1)
 
+    def half_to_sibling(h, oy, ox):
+        move(("s", h, oy % NY, ox % NX), oy, ox, lows[h], sizes[h], 0, 0, 1)
+
     def add_piece(oy, ox, oc):
         src = at_offset(-oy, -ox, oc)
         buf = piece(oy, ox, oc)
@@ -347,7 +350,11 @@
     def add(pieces, oc):
         for oy, ox in pieces:
             if oc:
-                moves["s", oy % NY, ox % NX].wait_recv()
+                if (oy, ox) in knight:
+                    for h in range(2):
+                        moves["s", h, oy % NY, ox % NX].wait_recv()
+                else:
+                    moves["s", oy % NY, ox % NX].wait_recv()
             add_piece(oy, ox, oc)
 
     for h in range(2):
@@ -381,10 +388,12 @@
         for s in (1, -1):
             moves["qf", h, 0, s].wait_recv()
     straight = [(0, 2), (2, 0)]
+    knight = [(1, 2), (-1, 2), (2, 1), (2, -1)]
     finish(straight)
     for s in (1, -1):
         for h in range(2):
             forward_second(h, 2, s)
+            half_to_sibling(h, *along(h, 2, s))
     z_wait_recv(cown, 3)
     lax.fori_loop(0, NG, build, 0)
     for pieces in ([(0, 0)], near, diagonal, straight):
@@ -394,8 +403,7 @@
         for h in range(2):
             for s in (1, -1):
                 moves["qf", h, i, s].wait_recv()
-    knight = [(1, 2), (-1, 2), (2, 1), (2, -1)]
-    finish(knight)
+            half_to_sibling(h, *along(h, i, 2))
     for n in range(NG - 1):
         for h in range(2):
             d_copy(n, h, False).wait_send()
@@ -404,14 +412,14 @@
     for h in range(2):
         z_wait_send(wz, 6 + 3 * h, (h, 2))
     z_wait_send(cown, 3)
-    add(knight, 0)
-    add(knight, 1)
     earlier = list(moves.values())
     for h in range(2):
         for s in (1, -1):
             moves["qf", h, 2, s].wait_recv()
         move(("s2", h), 2, 2, lows[h], sizes[h], 0, 0, 1)
+    add(knight, 0)
     add_piece(2, 2, 0)
+    add(knight, 1)
     for copy in earlier:
         copy.wait_send()
     for h in range(2):

time: 121 us -> 120 us (level)
  Pallas kernels: 119 us -> 117 us
    pallas_call x1, Pallas kernels: 117 us -> 116 us  [local(): lax.cond(few[0, 0] > 0, exchange(FEW, 0), exchange(TILES, 1), tab, keep,...]
where the time goes in v5:
time: 120 us
  Pallas kernels  117 us (98%)
  local copies, waits for them, and re-layouts  1.32 us (1%)
    pallas_call x1, Pallas kernels, local(): lax.cond(few[0, 0] > 0, exchange(FEW, 0), exchange(TILES, 1), tab, keep,...  116 us

profile of v5, /device:TPU:1, one launch (start us, length us, event | category | flops | bytes accessed | tf_op | source)
XLA Modules:
  0.0 119.5 jit_solution(11741796032021640364)
XLA Ops:
  0.0 1.6 %shard_map.66 = (s32[48,128]{1,0:T(8,128)S(1)}, f32[4,128]{1,0:T(4,128)S(1)}, s32[1,1]{1,0:T(1,128)}) custom-call(s32[8,128]{1,0:T(8,128)} %bitcast.3, s32[8,128]{1,0:T(8,128)} %bitcast.4), custom_call_target="tpu_custom_call" | custom-call | tf_op jit(solution)/shard_map/pallas_call | solution.py:435
  2.2 116.0 %conditional.1 = (f32[256,2048]{1,0:T(8,128)S(1)}) conditional(s32[]{:T(128)} %bitcast.2, (s32[48,128]{1,0:T(8,128)S(1)}, f32[4,128]{1,0:T(4,128)S(1)}, bf16[4,128,256]{2,1,0:T(8,128)(2,1)}, bf16[4,128,256]{2,1,0:T(8,128)(2,1)}, f32[4,128]{1,0:T(4,128)}, /*index=5*/bf16[256,8192]{1,0:T(8,128)(2,1)}) %tuple.11, (s32[48,128]{1,0:T(8,128)S(1)}, ...), branch_computations={%region_0.0_spmd, %region_1.0_spmd} | conditional | bytes 8 | solution.py:484
  2.4 115.8 %branch_1_fun.1 = f32[256,2048]{1,0:T(8,128)S(1)} custom-call(s32[48,128]{1,0:T(8,128)S(1)} %get-tuple-element.38.tab, f32[4,128]{1,0:T(4,128)S(1)} %get-tuple-element.39.keep, bf16[4,128,256]{2,1,0:T(8,128)(2,1)} %get-tuple-element.40.colloc, bf16[4,128,256]{2,1,0:T(8,128)(2,1)} %get-tuple-element.41.potent, f32[4,128]{1,0:T(4,128)} %get-tuple-element.42.weights, ...), custom_call_target="tpu_custom_call" | custom-call | tf_op jit(solution)/shard_map/cond/branch_1_fun/pallas_call | solution.py:484
  118.2 1.3 %copy.12 = f32[256,2048]{1,0:T(8,128)} copy(f32[256,2048]{1,0:T(8,128)S(1)} %get-tuple-element.50) | data formatting | bytes 4194304

commit v6 on v5

--- a/solution.py
+++ b/solution.py
@@ -17,6 +17,7 @@
 CAP = 2
 TILES = 16
 FEW = 13
+FEWER = 12
 N_COL = 64
 MESH = pl.DeviceIdType.MESH
 F32 = jnp.float32
@@ -124,7 +125,8 @@
     for z in range(NA):
         most = jnp.maximum(most, over_blocks(total((own // (NG // NA) == z).astype(i32))))
     most = jnp.where(block1 == 0, most, 0)
-    few[0, 0] = (jnp.max(most) <= FEW).astype(i32)
+    highest = jnp.max(most)
+    few[0, 0] = (highest <= FEW).astype(i32) + (highest <= FEWER).astype(i32)
 
 
 def kernel(count, tab, keep, colloc, potent, weights, dens, out, dtiles, send0, send1, arrived0, arrived1, cfull, cqs, cown, wz, lhs_t, picked, scaled, dloc, *rest):
@@ -481,10 +483,9 @@
             ),
         )
 
-    return lax.cond(
-        few[0, 0] > 0,
-        exchange(FEW, 0),
-        exchange(TILES, 1),
+    return lax.switch(
+        few[0, 0],
+        [exchange(TILES, 1), exchange(FEW, 0), exchange(FEWER, 2)],
         tab, keep, colloc, potent, weights, density,
     )
 

time: 120 us -> 117 us (0.975)
  Pallas kernels: 117 us -> 114 us
    pallas_call x1, Pallas kernels: 116 us -> 112 us  [local(): lax.switch(few[0, 0], [exchange(TILES, 1), exchange(FEW, 0), exchange(FEW...]
where the time goes in v6:
time: 117 us
  Pallas kernels  114 us (97%)
  local copies, waits for them, and re-layouts  1.32 us (1%)
    pallas_call x1, Pallas kernels, local(): lax.switch(few[0, 0], [exchange(TILES, 1), exchange(FEW, 0), exchange(FEW...  112 us

profile of v6, /device:TPU:1, one launch (start us, length us, event | category | flops | bytes accessed | tf_op | source)
XLA Modules:
  0.0 116.6 jit_solution(15857827090273218102)
XLA Ops:
  0.0 1.6 %shard_map.67 = (s32[48,128]{1,0:T(8,128)S(1)}, f32[4,128]{1,0:T(4,128)S(1)}, s32[1,1]{1,0:T(1,128)}) custom-call(s32[8,128]{1,0:T(8,128)} %bitcast.3, s32[8,128]{1,0:T(8,128)} %bitcast.4), custom_call_target="tpu_custom_call" | custom-call | tf_op jit(solution)/shard_map/pallas_call | solution.py:437
  2.2 113.0 %conditional.1 = (f32[256,2048]{1,0:T(8,128)S(1)}) conditional(s32[]{:T(128)} %bitcast.2, (s32[48,128]{1,0:T(8,128)S(1)}, f32[4,128]{1,0:T(4,128)S(1)}, bf16[4,128,256]{2,1,0:T(8,128)(2,1)}, bf16[4,128,256]{2,1,0:T(8,128)(2,1)}, f32[4,128]{1,0:T(4,128)}, /*index=5*/bf16[256,8192]{1,0:T(8,128)(2,1)}) %tuple.14, ...), branch_computations={%region_0.0_spmd, %region_1.0_spmd, %region_2.0_spmd} | conditional | bytes 8 | solution.py:486
  2.7 112.3 %branch_2_fun.1 = f32[256,2048]{1,0:T(8,128)S(1)} custom-call(s32[48,128]{1,0:T(8,128)S(1)} %get-tuple-element.57.tab, f32[4,128]{1,0:T(4,128)S(1)} %get-tuple-element.58.keep, bf16[4,128,256]{2,1,0:T(8,128)(2,1)} %get-tuple-element.59.colloc, bf16[4,128,256]{2,1,0:T(8,128)(2,1)} %get-tuple-element.60.potent, f32[4,128]{1,0:T(4,128)} %get-tuple-element.61.weights, ...), custom_call_target="tpu_custom_call" | custom-call | tf_op jit(solution)/shard_map/cond/branch_2_fun/pallas_call | solution.py:486
  115.3 1.3 %copy.14 = f32[256,2048]{1,0:T(8,128)} copy(f32[256,2048]{1,0:T(8,128)S(1)} %get-tuple-element.69) | data formatting | bytes 4194304
